TPU v7x, 256 devices: a whole 4x4x8 slice. The times are simulated.
256 devices in a mesh: polar: 32 (over z, y), azimuth: 8 (over x, core).
Axes of the slice: x: 4, y: 4, z: 8, core: 2. Of those that a mesh axis runs over, the one named last changes fastest.
Arguments:
- field: bfloat16 [768, 1440, 256], P('polar', 'azimuth'), may hold values from -6 to 6
- cotangent: bfloat16 [768, 1440, 256], P('polar', 'azimuth'), may hold values from -6 to 6
- legendre: bfloat16 [512, 768, 512], P(('polar', 'azimuth')), may hold values from -0.0625 to 0.0625, as said below
- lat_weight: float32 [768], replicated, may hold values from 0.5 to 2
- filter_weight: bfloat16 [512, 256, 256], P('polar'), may hold values from -0.375 to 0.375
- wave_order: int32 [512], replicated, may hold values from 0 to 511, as said below
- deg_order: int32 [64], replicated, may hold values from 0 to 63, as said below
Outputs:
- output: bfloat16 [768, 1440, 256], P('polar', 'azimuth')
- grad_field: bfloat16 [768, 1440, 256], P('polar', 'azimuth')
- grad_weight: float32 [512, 256, 256], P('polar', 'azimuth')
Inputs may be any that keep to these rules, and one draw needn't show every extreme that they name: `wave_order`: a permutation of the 512 wavenumbers; the 2 slots of one device (devices in polar+azimuth order) hold pairs m and 511 - m. `deg_order`: a permutation of the 64 degree blocks; the 2 block slots of one polar index hold pairs b and 63 - b. legendre[k, a, l] is 0 where l < wave_order[k].
All inputs are finite; a program needn't handle non-finite values.
Results may differ from a plain program's by a relative error of at most 0.023.
Values may be sent and summed in bfloat16 or wider, within the bound.
No kernel may reach another device: no remote copies, remote signals or barrier semaphores. Data moves between devices by JAX's collectives and lax.ppermute only.
A program may use at most 192 MiB of HBM per device.

v0:
```python
import functools
import math

import jax
import jax.numpy as jnp
from jax import lax
from jax.experimental import pallas as pl
from jax.experimental.pallas import tpu as pltpu
from jax.sharding import PartitionSpec as P

BF16 = jnp.bfloat16
F32 = jnp.float32
LANES = 128
ROW_PAD = 192
MIB = 1024 * 1024
WHOLE = 56
GELU_A = math.sqrt(2.0 / math.pi)
GELU_B = 0.044715


def exchange(payload, axes):
    return lax.all_to_all(payload, axes, split_axis=0, concat_axis=0, tiled=True)


def message_row(row, half, slot, part):
    return row * 8 + half * 4 + slot * 2 + part


def unpack_rows(received, wide, row, slot, part, peers):
    halves = [
        wide[pl.ds(message_row(row, half, slot, part), peers, stride=24), :] for half in range(2)
    ]
    return jnp.concatenate(halves, axis=1)


def doubling(zero_at, slot, peers):
    place = slot * peers + lax.broadcasted_iota(jnp.int32, (peers, LANES), 0)
    return jnp.where(place == zero_at, 1.0, 2.0)


def clear_pads(stage, across, lon):
    start = lon // 16 * 16
    for j in range(across):
        stage[j * ROW_PAD + start : (j + 1) * ROW_PAD, :] = jnp.zeros(
            (ROW_PAD - start, stage.shape[1]), BF16
        )


def dft_row(table, grid_rows, zero_at, wide, row, peers):
    total = jnp.dot(table[...], grid_rows[...], preferred_element_type=F32)
    for slot in range(2):
        for part in range(2):
            start = (slot * 2 + part) * peers
            for half in range(2):
                block = total[start : start + peers, half * LANES : (half + 1) * LANES]
                if zero_at is not None:
                    block = block * doubling(zero_at, slot, peers)
                wide[pl.ds(message_row(row, half, slot, part), peers, stride=24), :] = block


def dft_kernel(grid, table_back, out, wide, table, stages):
    across, rows, lon, _ = grid.shape
    peers = out.shape[0]
    table[...] = table_back[...].T
    for row in range(rows):
        stage = stages.at[row]
        clear_pads(stage, across, lon)
        for j in range(across):
            stage[j * ROW_PAD : j * ROW_PAD + lon, :] = grid[j, row]
        dft_row(table, stage, None, wide, row, peers)
    out[...] = wide[...].reshape(out.shape).astype(BF16)


def analysis_kernel(weighted, received, lat_w, folded_far, out, wide, columns, folded, arrival):
    fetch = pltpu.make_async_copy(folded_far, folded, arrival)
    fetch.start()
    peers = received.shape[0]
    wide[...] = received[...].astype(F32).reshape(wide.shape)
    rows = received.shape[1] // 8
    for slot in range(2):
        for row in range(rows):
            start = (slot * rows + row) * peers
            for part in range(2):
                for half in range(2):
                    block = wide[
                        pl.ds(message_row(row, half, slot, part), peers, stride=24), :
                    ]
                    if weighted:
                        block = block * lat_w[row * peers : (row + 1) * peers, :]
                    lane = (part * 2 + half) * LANES
                    columns[start : start + peers, lane : lane + LANES] = block.astype(BF16)
    fetch.wait()
    total = jnp.dot(folded[...], columns[...], preferred_element_type=F32).astype(BF16)
    groups = out.shape[0]
    for quarter in range(4):
        lanes = slice(quarter * LANES, (quarter + 1) * LANES)
        out[:, quarter * 16 : (quarter + 1) * 16, :] = total[:512, lanes].reshape(groups, 16, LANES)
    extra = total[512:528, :].astype(F32)
    tail = jnp.concatenate(
        [extra[0:1, q * LANES : (q + 1) * LANES] for q in range(4)]
        + [jnp.zeros((4, LANES), F32)],
        axis=0,
    )
    out[:, 64:72, :] = jnp.broadcast_to(tail.astype(BF16)[None], (groups, 8, LANES))


def synthesis_kernel(weighted, received, lat_w, spread, out, wide, degrees):
    peers = out.shape[0]
    groups = received.shape[0]
    rows = out.shape[1] // 8
    for quarter in range(4):
        lanes = slice(quarter * LANES, (quarter + 1) * LANES)
        degrees[:512, lanes] = received[:, quarter * 16 : (quarter + 1) * 16, :].reshape(512, LANES)
    tail = jnp.sum(received[...].astype(F32)[:, 64:72, :], axis=0)
    extra = jnp.concatenate([tail[q : q + 1, :] for q in range(4)], axis=1)
    first = lax.broadcasted_iota(jnp.int32, (128, 512), 0) == 0
    degrees[512:640, :] = jnp.where(first, extra, 0.0).astype(BF16)
    for slot in range(2):
        for row in range(rows):
            total = jnp.dot(
                spread[slot, row * peers : (row + 1) * peers, :],
                degrees[...],
                preferred_element_type=F32,
            )
            for part in range(2):
                for half in range(2):
                    lane = (part * 2 + half) * LANES
                    block = total[:, lane : lane + LANES]
                    if weighted:
                        block = block * lat_w[row * peers : (row + 1) * peers, :]
                    wide[pl.ds(message_row(row, half, slot, part), peers, stride=24), :] = block
    out[...] = wide[...].reshape(out.shape).astype(BF16)


def degree_rows(wide, index, groups):
    parts = []
    for part in range(2):
        halves = [
            wide[pl.ds((part * 2 + half) * 16 + index, groups, stride=72), :] for half in range(2)
        ]
        parts.append(jnp.concatenate(halves, axis=1))
    return jnp.concatenate(parts, axis=0)


def extra_rows(wide, groups):
    parts = []
    for part in range(2):
        halves = [
            wide[pl.ds(64 + part * 2 + half, groups, stride=72), :] for half in range(2)
        ]
        parts.append(jnp.concatenate(halves, axis=1))
    return jnp.concatenate(parts, axis=0)


def store_rows(wide, start_of, values, groups):
    for part in range(2):
        for half in range(2):
            wide[pl.ds(start_of(part * 2 + half), groups, stride=72), :] = values[
                part * groups : (part + 1) * groups, half * LANES : (half + 1) * LANES
            ]


def pair_masks(lowest, degree):
    partner = 511 - degree
    return (
        lowest >= 0,
        degree >= lowest,
        partner >= lowest,
        511 - lowest == degree,
        511 - lowest == partner,
    )


def lowest_waves(own, first, shape):
    column = lax.broadcasted_iota(jnp.int32, first.shape, 1) == own[0]
    lowest = jnp.sum(jnp.where(column, first[...], 0), axis=1, keepdims=True)
    return jnp.broadcast_to(jnp.concatenate([lowest, lowest], axis=0), shape)


def filter_kernel(own, blocks, received, weight, first, out, wide, result):
    groups = received.shape[0]
    wide[...] = received[...].astype(F32).reshape(wide.shape)
    result[...] = jnp.zeros_like(result)
    extra = extra_rows(wide, groups)
    lowest = lowest_waves(own, first, extra.shape)
    extra_sum = jnp.zeros_like(extra)
    for index in range(8):
        mirror = 15 - index
        degree = blocks[2 * own[1]] * 8 + index
        _, near, far, extra_near, extra_far = pair_masks(lowest, degree)
        one = degree_rows(wide, index, groups)
        two = degree_rows(wide, mirror, groups)
        stacked = jnp.concatenate([one, two, extra], axis=0).astype(BF16)
        by_one = jnp.dot(stacked, weight[index], preferred_element_type=F32)
        by_two = jnp.dot(stacked, weight[mirror], preferred_element_type=F32)
        side = 2 * groups
        store_rows(
            wide=result,
            start_of=lambda quarter: quarter * 16 + index,
            values=jnp.where(near, by_one[:side], by_two[:side]),
            groups=groups,
        )
        store_rows(
            wide=result,
            start_of=lambda quarter: quarter * 16 + mirror,
            values=jnp.where(far, by_two[side : 2 * side], by_one[side : 2 * side]),
            groups=groups,
        )
        extra_sum = (
            extra_sum
            + jnp.where(extra_near, by_one[2 * side :], 0.0)
            + jnp.where(extra_far, by_two[2 * side :], 0.0)
        )
    store_rows(result, lambda quarter: 64 + quarter, extra_sum, groups)
    out[...] = result[...].reshape(out.shape).astype(BF16)


def filter_back_kernel(
    own, blocks, received, weight, first, coeffs, out, grad_w, wide, result, wide_coeffs
):
    groups = received.shape[0]
    wide[...] = received[...].astype(F32).reshape(wide.shape)
    wide_coeffs[...] = coeffs[...].astype(F32).reshape(wide.shape)
    result[...] = jnp.zeros_like(result)
    extra = extra_rows(wide, groups)
    lowest = lowest_waves(own, first, extra.shape)
    extra_sum = jnp.zeros_like(extra)
    kept_extra = extra_rows(wide_coeffs, groups)
    turned = (((1,), (1,)), ((), ()))
    summed = (((0,), (0,)), ((), ()))
    for index in range(8):
        mirror = 15 - index
        degree = blocks[2 * own[1]] * 8 + index
        _, near, far, extra_near, extra_far = pair_masks(lowest, degree)
        one = degree_rows(wide, index, groups)
        two = degree_rows(wide, mirror, groups)
        stacked = jnp.concatenate([one, two, extra], axis=0).astype(BF16)
        kept_one = degree_rows(wide_coeffs, index, groups)
        kept_two = degree_rows(wide_coeffs, mirror, groups)
        kept_near = jnp.concatenate(
            [
                jnp.where(near, kept_one, 0.0),
                jnp.where(far, 0.0, kept_two),
                jnp.where(extra_near, kept_extra, 0.0),
            ],
            axis=0,
        ).astype(BF16)
        kept_far = jnp.concatenate(
            [
                jnp.where(near, 0.0, kept_one),
                jnp.where(far, kept_two, 0.0),
                jnp.where(extra_far, kept_extra, 0.0),
            ],
            axis=0,
        ).astype(BF16)
        for place, kept in ((index, kept_near), (mirror, kept_far)):
            grad_w[place] = lax.dot_general(
                kept, stacked, summed, preferred_element_type=F32
            ).astype(BF16)
        by_one = lax.dot_general(stacked, weight[index], turned, preferred_element_type=F32)
        by_two = lax.dot_general(stacked, weight[mirror], turned, preferred_element_type=F32)
        side = 2 * groups
        store_rows(
            wide=result,
            start_of=lambda quarter: quarter * 16 + index,
            values=jnp.where(near, by_one[:side], by_two[:side]),
            groups=groups,
        )
        store_rows(
            wide=result,
            start_of=lambda quarter: quarter * 16 + mirror,
            values=jnp.where(far, by_two[side : 2 * side], by_one[side : 2 * side]),
            groups=groups,
        )
        extra_sum = (
            extra_sum
            + jnp.where(extra_near, by_one[2 * side :], 0.0)
            + jnp.where(extra_far, by_two[2 * side :], 0.0)
        )
    store_rows(result, lambda quarter: 64 + quarter, extra_sum, groups)
    out[...] = result[...].reshape(out.shape).astype(BF16)


def idft_row(table_back, wide, zero_at, row, peers, linear):
    pieces = []
    for slot in range(2):
        for part in range(2):
            halves = []
            for half in range(2):
                block = wide[pl.ds(message_row(row, half, slot, part), peers, stride=24), :]
                if zero_at is not None:
                    block = block * doubling(zero_at, slot, peers)
                halves.append(block.astype(BF16))
            pieces.append(jnp.concatenate(halves, axis=1))
    spectrum = jnp.concatenate(pieces, axis=0)
    linear[...] = jnp.dot(table_back[...], spectrum, preferred_element_type=F32)


def middle_kernel(own, received, table_back, grid_far, *refs):
    across, rows, lon, _ = grid_far.shape
    cot_far, spectrum, out_far = refs[:across], refs[across], refs[across + 1]
    wide, table, grid, cotangent, output, stages, linears = refs[across + 2 : across + 9]
    grid_in, cot_in, leaving = refs[across + 9 :]
    others = [pltpu.make_async_copy(grid_far, grid, grid_in)] + [
        pltpu.make_async_copy(cot_far[k], cotangent.at[own[0] ^ k], cot_in.at[k])
        for k in range(across)
    ]
    for copy in others:
        copy.start()
    zero_at = own[2]
    peers = received.shape[0]
    wide[...] = received[...].astype(F32).reshape(wide.shape)
    for row in range(rows):
        clear_pads(stages.at[row], across, lon)
        idft_row(table_back, wide, zero_at, row, peers, linears.at[row])
    table[...] = table_back[...].T
    for copy in others:
        copy.wait()
    leave = [
        pltpu.make_async_copy(output.at[row], out_far.at[:, row], leaving.at[row])
        for row in range(rows)
    ]
    for row in range(rows):
        linear, stage = linears.at[row], stages.at[row]
        for j in range(across):
            place = slice(j * ROW_PAD, j * ROW_PAD + lon)
            value = linear[place, :].astype(BF16).astype(F32)
            square = value * value
            bend = jnp.tanh(value * (GELU_A + (GELU_A * GELU_B) * square))
            gate = 0.5 + 0.5 * bend
            output[row, j] = (grid[j, row].astype(F32) + value * gate).astype(BF16)
            steep = value * (2.0 * GELU_A + (6.0 * GELU_A * GELU_B) * square)
            slope = gate + steep * (gate - gate * gate)
            stage[place, :] = (cotangent[j, row].astype(F32) * slope).astype(BF16)
        leave[row].start()
        dft_row(table, stage, zero_at, wide, row, peers)
    spectrum[...] = wide[...].reshape(spectrum.shape).astype(BF16)
    for copy in leave:
        copy.wait()


def last_kernel(own, received, table_back, *refs):
    across = len(refs) - 7
    cot_far, out_far = refs[:across], refs[across]
    wide, cotangent, output, linears, cot_in, leaving = refs[across + 1 :]
    _, rows, lon, _ = out_far.shape
    others = [
        pltpu.make_async_copy(cot_far[k], cotangent.at[own[0] ^ k], cot_in.at[k])
        for k in range(across)
    ]
    for copy in others:
        copy.start()
    peers = received.shape[0]
    wide[...] = received[...].astype(F32).reshape(wide.shape)
    leave = [
        pltpu.make_async_copy(output.at[row], out_far.at[:, row], leaving.at[row])
        for row in range(rows)
    ]
    for row in range(rows):
        linear = linears.at[row]
        idft_row(table_back, wide, None, row, peers, linear)
        if row == 0:
            for copy in others:
                copy.wait()
        for j in range(across):
            value = linear[j * ROW_PAD : j * ROW_PAD + lon, :].astype(BF16).astype(F32)
            output[row, j] = (cotangent[j, row].astype(F32) + value).astype(BF16)
        leave[row].start()
    for copy in leave:
        copy.wait()


def split_kernel(grid, *refs):
    lon, lat, _ = grid.shape
    wide = refs[-1]
    wide[...] = grid[...].astype(F32).reshape(wide.shape)
    across, rows = refs[0].shape[:2]
    for j in range(across):
        for row in range(rows):
            refs[0][j, row] = wide[pl.ds(row * across + j, lon, stride=lat), :].astype(BF16)


def split_far_kernel(own, grid, *refs):
    lon, lat, channels = grid.shape
    across = len(refs) - 3
    outs, (wide, bands, leaving) = refs[:across], refs[across:]
    rows = outs[0].shape[0]
    for lane in range(0, channels, LANES):
        lanes = slice(lane, lane + LANES)
        wide[...] = grid[:, :, lanes].astype(F32).reshape(wide.shape)
        for k in range(across):
            for row in range(rows):
                start = row * across + (own[0] ^ k)
                bands[k, row, :, lanes] = wide[pl.ds(start, lon, stride=lat), :].astype(BF16)
    copies = [
        pltpu.make_async_copy(bands.at[k], outs[k], leaving.at[k]) for k in range(across)
    ]
    for copy in copies:
        copy.start()
    for copy in copies:
        copy.wait()


def join_kernel(own, *refs):
    bands, out, wide = refs[:-2], refs[-2], refs[-1]
    lon, lat, _ = out.shape
    across, rows = len(bands), bands[0].shape[0]
    for k in range(across):
        for row in range(rows):
            start = row * across + (own[0] ^ k)
            wide[pl.ds(start, lon, stride=lat), :] = bands[k][row].astype(F32)
    out[...] = wide[...].reshape(out.shape).astype(BF16)


def degree_tables_kernel(own, blocks, waves, legendre, folded, spread, ordered, chosen):
    slots, lat_all, degree_count = legendre.shape
    count = degree_count // 16
    own_waves = [waves[own[3] * slots + slot] for slot in range(slots)]
    step = lax.broadcasted_iota(jnp.int32, (8, degree_count), 0)
    lane = lax.broadcasted_iota(jnp.int32, (8, degree_count), 1)
    chosen[...] = jnp.zeros_like(chosen)
    for pair in range(count):
        for slot in range(slots):
            pieces = []
            for block in (2 * pair, 2 * pair + 1):
                degree = blocks[block] * 8 + step
                if slot:
                    degree = jnp.where(
                        degree == own_waves[0], degree_count, degree_count - 1 - degree
                    )
                pieces.append(jnp.where(degree == lane, 1.0, 0.0))
            chosen[slot, pair * 16 : (pair + 1) * 16, :] = jnp.concatenate(pieces, axis=0).astype(
                BF16
            )
    sixteen = lax.broadcasted_iota(jnp.int32, (16, degree_count), 0)
    lanes = lax.broadcasted_iota(jnp.int32, (16, degree_count), 1)
    last = jnp.where(jnp.logical_and(sixteen == 0, lanes == own_waves[1]), 1.0, 0.0)
    chosen[1, degree_count : degree_count + 16, :] = last.astype(BF16)
    turned = (((1,), (1,)), ((), ()))
    for slot in range(slots):
        plane = legendre[slot].astype(F32).reshape(-1, lat_all // 256, 8, degree_count)
        for row in range(lat_all // 256):
            ordered[row * 256 : (row + 1) * 256, :] = (
                plane[:, row].reshape(256, degree_count).astype(BF16)
            )
        spread[slot] = lax.dot_general(
            ordered[...], chosen[slot], turned, preferred_element_type=F32
        ).astype(BF16)
        folded[:, slot * lat_all : (slot + 1) * lat_all] = lax.dot_general(
            chosen[slot, : degree_count + 16, :], ordered[...], turned, preferred_element_type=F32
        ).astype(BF16)


def tables(waves, lon_count, across):
    block = lon_count // across
    place = jnp.arange(ROW_PAD, dtype=jnp.int32)[:, None]
    angle = (2.0 * math.pi / lon_count) * (place * waves[None, :] % lon_count).astype(F32)
    size = jnp.where(place < block, 1.0 / math.sqrt(lon_count), 0.0)
    cosine, sine = jnp.cos(angle) * size, jnp.sin(angle) * size
    turn = jnp.arange(across, dtype=jnp.int32)[:, None] * waves[None, :] % across
    turn = (2.0 * math.pi / across) * turn.astype(F32)
    turn_cos, turn_sin = jnp.cos(turn)[:, None, :], jnp.sin(turn)[:, None, :]
    real = (cosine * turn_cos - sine * turn_sin).astype(BF16)
    imag = -(sine * turn_cos + cosine * turn_sin).astype(BF16)
    half = waves.shape[0] // 2
    back = jnp.concatenate(
        [real[..., :half], imag[..., :half], real[..., half:], imag[..., half:]], axis=-1
    )
    return back.reshape(across * ROW_PAD, 2 * waves.shape[0])


def body(field, cotangent, legendre, lat_weight, filter_weight, wave_order, deg_order):
    polar_count = lax.axis_size("polar")
    across = lax.axis_size("azimuth")
    peers = polar_count * across
    both = ("polar", "azimuth")
    lat_rows, lon_cols, channels = field.shape
    rows = lat_rows // across
    slots, lat_all, degree_count = legendre.shape
    block_size = degree_count // deg_order.shape[0]
    polar, azimuth = lax.axis_index("polar"), lax.axis_index("azimuth")
    device = polar * across + azimuth
    lon_count = lon_cols * across

    vmem = pl.BlockSpec(memory_space=pltpu.VMEM)
    smem = pl.BlockSpec(memory_space=pltpu.SMEM)
    far = pl.BlockSpec(memory_space=pltpu.HBM)
    pairs = wave_order.reshape(peers, slots)
    waves = pairs.T.reshape(-1)
    zero_at = jnp.sum(jnp.where(waves == 0, jnp.arange(waves.shape[0], dtype=jnp.int32), 0))
    own = jnp.stack([azimuth, polar, zero_at, device])
    band = (rows, lon_cols, channels)
    bands_shape = (across, *band)
    one_band = jax.ShapeDtypeStruct(band, BF16)
    trade = [[(i, i ^ k) for i in range(across)] for k in range(across)]

    def kernel_call(kernel, outs, in_specs, out_specs, scratch, mib, cost, *operands):
        return pl.pallas_call(
            kernel,
            out_shape=outs,
            in_specs=in_specs,
            out_specs=out_specs,
            scratch_shapes=scratch,
            compiler_params=pltpu.CompilerParams(vmem_limit_bytes=mib * MIB),
            cost_estimate=pl.CostEstimate(
                flops=cost, bytes_accessed=cost // 1000, transcendentals=0
            ),
        )(*operands)

    def half_bands(kernel, ins, outs, scalars, *operands):
        def spec(array):
            inner = tuple(array.shape[:-1])
            return pl.BlockSpec((*inner, LANES), lambda h: (0,) * len(inner) + (h,))

        return pl.pallas_call(
            kernel,
            grid=(channels // LANES,),
            out_shape=outs,
            in_specs=[smem] * len(scalars) + [spec(x) for x in ins],
            out_specs=jax.tree.map(spec, outs),
            scratch_shapes=[pltpu.VMEM((lon_cols * lat_rows, LANES), F32)],
            compiler_params=pltpu.CompilerParams(vmem_limit_bytes=56 * MIB),
            cost_estimate=pl.CostEstimate(flops=2_000, bytes_accessed=2_000, transcendentals=0),
        )(*scalars, *operands)

    def join_bands(bands):
        out = jax.ShapeDtypeStruct((lon_cols, lat_rows, channels), BF16)
        return jnp.transpose(half_bands(join_kernel, bands, out, [own], *bands), (1, 0, 2))

    def piece(bands, k):
        if isinstance(bands, (list, tuple)):
            return bands[k]
        return lax.dynamic_index_in_dim(bands, azimuth ^ k, 0, keepdims=False)

    def beside(payload, axes, bands, kinds, done):
        payload, bands = lax.optimization_barrier((payload, bands))
        moved = [lax.ppermute(piece(bands, k), "azimuth", trade[k]) for k in kinds]
        payload = exchange(payload, axes)
        payload, bands, moved = lax.optimization_barrier((payload, bands, moved))
        done.update(zip(kinds, moved))
        return payload, bands

    groups = ((2, 6, 4), (1, 3, 7, 5))

    turned_field = jnp.transpose(field, (1, 0, 2))
    grid = exchange(
        half_bands(
            split_kernel,
            [turned_field],
            jax.ShapeDtypeStruct(bands_shape, BF16),
            [],
            turned_field,
        ),
        "azimuth",
    )

    table_back = tables(waves, lon_count, across)
    folded, spread = kernel_call(
        degree_tables_kernel,
        (
            jax.ShapeDtypeStruct((degree_count + 16, slots * lat_all), BF16),
            jax.ShapeDtypeStruct((slots, lat_all, degree_count + LANES), BF16),
        ),
        [smem, smem, smem, vmem],
        (vmem, vmem),
        [
            pltpu.VMEM((lat_all, degree_count), BF16),
            pltpu.VMEM((slots, degree_count + LANES, degree_count), BF16),
        ],
        32,
        1000,
        own,
        deg_order,
        wave_order,
        legendre,
    )
    lat_w = jnp.broadcast_to(
        lat_weight.reshape(polar_count, rows, across).transpose(1, 0, 2).reshape(-1, 1),
        (lat_all, LANES),
    )
    first = pairs[:, 0].reshape(polar_count, across)
    cot_send = kernel_call(
        split_far_kernel,
        (one_band,) * across,
        [smem, vmem],
        (far,) * across,
        [
            pltpu.VMEM((lon_cols * lat_rows, LANES), F32),
            pltpu.VMEM(bands_shape, BF16),
            pltpu.SemaphoreType.DMA((across,)),
        ],
        24,
        1000,
        own,
        jnp.transpose(cotangent, (1, 0, 2)),
    )
    grid, table_back, folded, spread, lat_w, first, cot_send = lax.optimization_barrier(
        (grid, table_back, folded, spread, lat_w, first, cot_send)
    )

    message = (peers, 8 * rows, LANES)
    degree_message = (polar_count, 72, LANES)
    wide = pltpu.VMEM((peers * 8 * rows, LANES), F32)
    degree_wide = pltpu.VMEM((polar_count * 72, LANES), F32)
    stages = pltpu.VMEM((rows, across * ROW_PAD, channels), BF16)
    linears = pltpu.VMEM((rows, across * ROW_PAD, channels), F32)
    held_bands = pltpu.VMEM(bands_shape, BF16)
    held_rows = pltpu.VMEM((rows, across, lon_cols, channels), BF16)
    sems = pltpu.SemaphoreType.DMA
    held_table = pltpu.VMEM(table_back.shape[::-1], BF16)
    spectrum_shape = jax.ShapeDtypeStruct(message, BF16)
    degree_shape = jax.ShapeDtypeStruct(degree_message, BF16)
    local_degrees = filter_weight.shape[0]

    def analysis(received, weighted):
        return kernel_call(
            functools.partial(analysis_kernel, weighted),
            degree_shape,
            [vmem, vmem, far],
            vmem,
            [
                wide,
                pltpu.VMEM((slots * lat_all, 4 * LANES), BF16),
                pltpu.VMEM(folded.shape, BF16),
                sems,
            ],
            24,
            800_000_000,
            received,
            lat_w,
            folded,
        )

    def synthesis(received, weighted):
        return kernel_call(
            functools.partial(synthesis_kernel, weighted),
            spectrum_shape,
            [vmem] * 3,
            vmem,
            [wide, pltpu.VMEM((degree_count + LANES, 4 * LANES), BF16)],
            24,
            800_000_000,
            received,
            lat_w,
            spread,
        )

    spectrum = kernel_call(
        dft_kernel,
        spectrum_shape,
        [vmem, vmem],
        vmem,
        [wide, held_table, stages],
        WHOLE,
        2_400_000_000,
        grid,
        table_back,
    )
    cot_bands = {0: cot_send[0]}
    arrived, cot_send = beside(spectrum, both, cot_send, groups[0], cot_bands)
    coeffs = analysis(arrived, True)
    coeffs, cot_send = beside(coeffs, "polar", cot_send, groups[1], cot_bands)
    filtered = kernel_call(
        filter_kernel,
        degree_shape,
        [smem, smem, vmem, vmem, vmem],
        vmem,
        [degree_wide, degree_wide],
        24,
        300_000_000,
        own,
        deg_order,
        coeffs,
        filter_weight,
        first,
    )
    filtered = exchange(filtered, "polar")
    cot_bands = [cot_bands[k] for k in range(across)]
    arrived = exchange(synthesis(filtered, False), both)
    grad_spec, output_bands = kernel_call(
        middle_kernel,
        (spectrum_shape, jax.ShapeDtypeStruct(bands_shape, BF16)),
        [smem, vmem, vmem] + [far] * (1 + across),
        (vmem, far),
        [
            wide,
            held_table,
            held_bands,
            held_bands,
            held_rows,
            stages,
            linears,
            sems,
            sems((across,)),
            sems((rows,)),
        ],
        WHOLE,
        4_800_000_000,
        own,
        arrived,
        table_back,
        grid,
        *cot_bands,
    )
    output_moved = {}
    arrived, output_bands = beside(grad_spec, both, output_bands, groups[0], output_moved)
    grad_filtered = analysis(arrived, False)
    grad_filtered, output_bands = beside(
        grad_filtered, "polar", output_bands, groups[1], output_moved
    )
    grad_coeffs, weight_terms = kernel_call(
        filter_back_kernel,
        (degree_shape, jax.ShapeDtypeStruct(filter_weight.shape, BF16)),
        [smem, smem, vmem, vmem, vmem, vmem],
        (vmem, vmem),
        [degree_wide, degree_wide, degree_wide],
        24,
        600_000_000,
        own,
        deg_order,
        grad_filtered,
        filter_weight,
        first,
        coeffs,
    )
    grad_coeffs = exchange(grad_coeffs, "polar")
    output_moved[0] = piece(output_bands, 0)
    grad_weight = lax.psum_scatter(
        weight_terms, "azimuth", scatter_dimension=1, tiled=True
    ).astype(F32)
    arrived = exchange(synthesis(grad_coeffs, True), both)
    grad_bands = kernel_call(
        last_kernel,
        jax.ShapeDtypeStruct(bands_shape, BF16),
        [smem, vmem, vmem] + [far] * across,
        far,
        [wide, held_bands, held_rows, linears, sems((across,)), sems((rows,))],
        WHOLE,
        2_400_000_000,
        own,
        arrived,
        table_back,
        *cot_bands,
    )
    output_moved = [output_moved[k] for k in range(across)]
    grad_bands, output_moved = lax.optimization_barrier((grad_bands, output_moved))
    output = join_bands(output_moved)
    grad_field = (
        exchange(grad_bands, "azimuth")
        .transpose(1, 0, 2, 3)
        .reshape(lat_rows, lon_cols, channels)
    )
    return (output, grad_field, grad_weight)


def solution(mesh):
    placed = (
        P("polar", "azimuth", None),
        P("polar", "azimuth", None),
        P(("polar", "azimuth"), None, None),
        P(),
        P("polar", None, None),
        P(),
        P(),
    )
    return jax.shard_map(
        body,
        mesh=mesh,
        in_specs=placed,
        out_specs=(
            P("polar", "azimuth", None),
            P("polar", "azimuth", None),
            P("polar", "azimuth", None),
        ),
        check_vma=False,
    )
```

profile of v0, /device:TPU:1, one launch (start us, length us, event | category | flops | bytes accessed | tf_op | source)
XLA Modules:
  0.0 444.5 jit_solution(6852729714787958244)
XLA Ops:
  7.2 3.6 shard_map.94
  10.8 7.6 %all-to-all-start = ((bf16[8,3,180,256]{3,2,1,0:T(8,128)(2,1)}), bf16[8,3,180,256]{3,2,1,0:T(8,128)(2,1)}, u32[]{:S(2)}, u32[]{:S(2)}) async-start(bf16[8,3,180,256]{3,2,1,0:T(8,128)(2,1)} %shard_map.94), calls=%async_computation | async-start | bytes 4521984 | tf_op jit(solution)/shard_map/all_to_all | solution.py:22
  36.1 10.4 %all-to-all-done.grid.grid_far = bf16[8,3,180,256]{3,2,1,0:T(8,128)(2,1)} async-done(((bf16[8,3,180,256]{3,2,1,0:T(8,128)(2,1)}), bf16[8,3,180,256]{3,2,1,0:T(8,128)(2,1)}, u32[]{:S(2)}, u32[]{:S(2)}) %all-to-all-start) | async-done | bytes 2211872 | tf_op jit(solution)/shard_map/all_to_all | solution.py:22
  46.7 6.8 %shard_map.97 = bf16[256,24,128]{2,1,0:T(8,128)(2,1)} custom-call(bf16[8,3,180,256]{3,2,1,0:T(8,128)(2,1)} %all-to-all-done.grid.grid_far, bf16[1536,1024]{1,0:T(8,128)(2,1)} %bitcast.34), custom_call_target="tpu_custom_call" | custom-call | flops 2400000000 | bytes 2400000 | tf_op jit(solution)/shard_map/pallas_call | solution.py:498
  53.5 12.3 %all-to-all-start.1 = ((bf16[256,24,128]{2,1,0:T(8,128)(2,1)}), bf16[256,24,128]{2,1,0:T(8,128)(2,1)}, u32[]{:S(2)}, u32[]{:S(2)}) async-start(bf16[256,24,128]{2,1,0:T(8,128)(2,1)} %shard_map.97), calls=%async_computation.1 | async-start | bytes 3145728 | tf_op jit(solution)/shard_map/all_to_all | solution.py:22
  69.7 8.1 %collective-permute-done.refs_2_ = bf16[3,180,256]{2,1,0:T(8,128)(2,1)S(1)} collective-permute-done((bf16[3,180,256]{2,1,0:T(8,128)(2,1)}, bf16[3,180,256]{2,1,0:T(8,128)(2,1)S(1)}, u32[]{:S(2)}, u32[]{:S(2)}) %collective-permute-start) | collective-permute-done | bytes 276512 | tf_op jit(solution)/shard_map/ppermute | solution.py:537
  77.9 3.7 collective-permute-done.1.refs_6_
  82.3 9.2 %collective-permute-done.2.refs_4_ = bf16[3,180,256]{2,1,0:T(8,128)(2,1)} collective-permute-done((bf16[3,180,256]{2,1,0:T(8,128)(2,1)S(1)}, bf16[3,180,256]{2,1,0:T(8,128)(2,1)}, u32[]{:S(2)}, u32[]{:S(2)}) %collective-permute-start.2) | collective-permute-done | bytes 276512 | tf_op jit(solution)/shard_map/ppermute | solution.py:537
  91.4 15.4 %all-to-all-done.1.received = bf16[256,24,128]{2,1,0:T(8,128)(2,1)} async-done(((bf16[256,24,128]{2,1,0:T(8,128)(2,1)}), bf16[256,24,128]{2,1,0:T(8,128)(2,1)}, u32[]{:S(2)}, u32[]{:S(2)}) %all-to-all-start.1) | async-done | bytes 1572896 | tf_op jit(solution)/shard_map/all_to_all | solution.py:22
  108.2 3.7 shard_map.98
  112.7 5.0 %all-to-all-start.2 = ((bf16[32,72,128]{2,1,0:T(8,128)(2,1)}), bf16[32,72,128]{2,1,0:T(8,128)(2,1)S(1)}, u32[]{:S(2)}, u32[]{:S(2)}) async-start(bf16[32,72,128]{2,1,0:T(8,128)(2,1)} %copy-done.8), calls=%async_computation.2 | async-start | bytes 1179648 | tf_op jit(solution)/shard_map/all_to_all | solution.py:22
  122.7 6.1 %collective-permute-done.4.refs_3_ = bf16[3,180,256]{2,1,0:T(8,128)(2,1)S(1)} collective-permute-done((bf16[3,180,256]{2,1,0:T(8,128)(2,1)}, bf16[3,180,256]{2,1,0:T(8,128)(2,1)S(1)}, u32[]{:S(2)}, u32[]{:S(2)}) %collective-permute-start.4) | collective-permute-done | bytes 276512 | tf_op jit(solution)/shard_map/ppermute | solution.py:537
  128.8 7.2 %collective-permute-done.5.refs_7_ = bf16[3,180,256]{2,1,0:T(8,128)(2,1)S(1)} collective-permute-done((bf16[3,180,256]{2,1,0:T(8,128)(2,1)}, bf16[3,180,256]{2,1,0:T(8,128)(2,1)S(1)}, u32[]{:S(2)}, u32[]{:S(2)}) %collective-permute-start.5) | collective-permute-done | bytes 276512 | tf_op jit(solution)/shard_map/ppermute | solution.py:537
  138.1 26.6 %all_to_all.50.received = bf16[32,72,128]{2,1,0:T(8,128)(2,1)S(1)} all-to-all(bf16[32,72,128]{2,1,0:T(8,128)(2,1)S(1)} %shard_map.99), channel_id=1, replica_groups=mesh['polar'=32,'azimuth'=8] {'polar'}, dimensions={0} | all-to-all | bytes 1179648 | tf_op jit(solution)/shard_map/all_to_all | solution.py:22
  166.4 49.9 %all_to_all.51.received = bf16[256,24,128]{2,1,0:T(8,128)(2,1)} all-to-all(bf16[256,24,128]{2,1,0:T(8,128)(2,1)S(1)} %shard_map.100), channel_id=1, replica_groups=mesh['polar'=32,'azimuth'=8] {'polar','azimuth'}, dimensions={0} | all-to-all | bytes 3145728 | tf_op jit(solution)/shard_map/all_to_all | solution.py:22
  216.3 13.0 %shard_map.101 = (bf16[256,24,128]{2,1,0:T(8,128)(2,1)}, bf16[8,3,180,256]{3,2,1,0:T(8,128)(2,1)}) custom-call(s32[4]{0:T(128)} %copy-done.12, bf16[256,24,128]{2,1,0:T(8,128)(2,1)} %all_to_all.51.received, bf16[1536,1024]{1,0:T(8,128)(2,1)} %bitcast.35, bf16[8,3,180,256]{3,2,1,0:T(8,128)(2,1)} %all-to-all-done.grid.grid_far, ...), custom_call_target="tpu_custom_call" | custom-call | flops 4800000000 | bytes 4800000 | tf_op jit(solution)/shard_map/pallas_call | solution.py:498
  229.3 7.9 %all-to-all-start.5 = ((bf16[256,24,128]{2,1,0:T(8,128)(2,1)}), bf16[256,24,128]{2,1,0:T(8,128)(2,1)}, u32[]{:S(2)}, u32[]{:S(2)}) async-start(bf16[256,24,128]{2,1,0:T(8,128)(2,1)} %get-tuple-element.129), calls=%async_computation.5 | async-start | bytes 3145728 | tf_op jit(solution)/shard_map/all_to_all | solution.py:22
  242.6 7.1 %collective-permute-done.7.refs_2_ = bf16[3,180,256]{2,1,0:T(8,128)(2,1)S(1)} collective-permute-done((bf16[3,180,256]{2,1,0:T(8,128)(2,1)S(1)}, bf16[3,180,256]{2,1,0:T(8,128)(2,1)S(1)}, u32[]{:S(2)}, u32[]{:S(2)}) %collective-permute-start.7) | collective-permute-done | bytes 276512 | tf_op jit(solution)/shard_map/ppermute | solution.py:537
  249.7 12.6 %collective-permute-done.8.refs_6_ = bf16[3,180,256]{2,1,0:T(8,128)(2,1)S(1)} collective-permute-done((bf16[3,180,256]{2,1,0:T(8,128)(2,1)S(1)}, bf16[3,180,256]{2,1,0:T(8,128)(2,1)S(1)}, u32[]{:S(2)}, u32[]{:S(2)}) %collective-permute-start.8) | collective-permute-done | bytes 276512 | tf_op jit(solution)/shard_map/ppermute | solution.py:537
  264.3 13.8 %all-to-all-done.5.received = bf16[256,24,128]{2,1,0:T(8,128)(2,1)} async-done(((bf16[256,24,128]{2,1,0:T(8,128)(2,1)}), bf16[256,24,128]{2,1,0:T(8,128)(2,1)}, u32[]{:S(2)}, u32[]{:S(2)}) %all-to-all-start.5) | async-done | bytes 1572896 | tf_op jit(solution)/shard_map/all_to_all | solution.py:22
  279.5 3.4 shard_map.102
  283.8 5.3 %all-to-all-start.6 = ((bf16[32,72,128]{2,1,0:T(8,128)(2,1)}), bf16[32,72,128]{2,1,0:T(8,128)(2,1)}, u32[]{:S(2)}, u32[]{:S(2)}) async-start(bf16[32,72,128]{2,1,0:T(8,128)(2,1)} %copy-done.7), calls=%async_computation.6 | async-start | bytes 1179648 | tf_op jit(solution)/shard_map/all_to_all | solution.py:22
  295.4 5.9 %collective-permute-done.11.refs_3_ = bf16[3,180,256]{2,1,0:T(8,128)(2,1)S(1)} collective-permute-done((bf16[3,180,256]{2,1,0:T(8,128)(2,1)S(1)}, bf16[3,180,256]{2,1,0:T(8,128)(2,1)S(1)}, u32[]{:S(2)}, u32[]{:S(2)}) %collective-permute-start.11) | collective-permute-done | bytes 276512 | tf_op jit(solution)/shard_map/ppermute | solution.py:537
  301.2 7.3 %collective-permute-done.12.refs_7_ = bf16[3,180,256]{2,1,0:T(8,128)(2,1)S(1)} collective-permute-done((bf16[3,180,256]{2,1,0:T(8,128)(2,1)S(1)}, bf16[3,180,256]{2,1,0:T(8,128)(2,1)S(1)}, u32[]{:S(2)}, u32[]{:S(2)}) %collective-permute-start.12) | collective-permute-done | bytes 276512 | tf_op jit(solution)/shard_map/ppermute | solution.py:537
  309.3 4.3 shard_map.103
  313.6 27.5 %all_to_all.52.received = bf16[32,72,128]{2,1,0:T(8,128)(2,1)S(1)} all-to-all(bf16[32,72,128]{2,1,0:T(8,128)(2,1)S(1)} %get-tuple-element.136), channel_id=1, replica_groups=mesh['polar'=32,'azimuth'=8] {'polar'}, dimensions={0} | all-to-all | bytes 1179648 | tf_op jit(solution)/shard_map/all_to_all | solution.py:22
  344.1 7.6 %all-to-all-start.8 = ((bf16[256,24,128]{2,1,0:T(8,128)(2,1)}), bf16[256,24,128]{2,1,0:T(8,128)(2,1)S(1)}, u32[]{:S(2)}, u32[]{:S(2)}) async-start(bf16[256,24,128]{2,1,0:T(8,128)(2,1)} %shard_map.104), calls=%async_computation.8 | async-start | bytes 3145728 | tf_op jit(solution)/shard_map/all_to_all | solution.py:22
  354.1 39.3 %all-to-all-done.8.received = bf16[256,24,128]{2,1,0:T(8,128)(2,1)S(1)} async-done(((bf16[256,24,128]{2,1,0:T(8,128)(2,1)}), bf16[256,24,128]{2,1,0:T(8,128)(2,1)S(1)}, u32[]{:S(2)}, u32[]{:S(2)}) %all-to-all-start.8) | async-done | bytes 1572896 | tf_op jit(solution)/shard_map/all_to_all | solution.py:22
  394.5 7.4 %shard_map.105 = bf16[8,3,180,256]{3,2,1,0:T(8,128)(2,1)} custom-call(s32[4]{0:T(128)} %copy-done.12, bf16[256,24,128]{2,1,0:T(8,128)(2,1)} %copy-done.22, bf16[1536,1024]{1,0:T(8,128)(2,1)} %bitcast.36, bf16[3,180,256]{2,1,0:T(8,128)(2,1)} %copy-done.11, bf16[3,180,256]{2,1,0:T(8,128)(2,1)} %copy-done.25, bf16[3,180,256]{2,1,0:T(8,128)(2,1)} %copy-done.23, ...), custom_call_target="tpu_custom_call" | custom-call | flops 2400000000 | bytes 2400000 | tf_op jit(solution)/shard_map/pallas_call | solution.py:498
  401.9 5.4 %all-to-all-start.9 = ((bf16[8,3,180,256]{3,2,1,0:T(8,128)(2,1)}), bf16[8,3,180,256]{3,2,1,0:T(8,128)(2,1)S(1)}, u32[]{:S(2)}, u32[]{:S(2)}) async-start(bf16[8,3,180,256]{3,2,1,0:T(8,128)(2,1)} %shard_map.105), calls=%async_computation.9 | async-start | bytes 4521984 | tf_op jit(solution)/shard_map/all_to_all | solution.py:22
  409.1 3.8 shard_map.106
  412.9 22.5 %all-to-all-done.9 = bf16[8,3,180,256]{3,2,1,0:T(8,128)(2,1)S(1)} async-done(((bf16[8,3,180,256]{3,2,1,0:T(8,128)(2,1)}), bf16[8,3,180,256]{3,2,1,0:T(8,128)(2,1)S(1)}, u32[]{:S(2)}, u32[]{:S(2)}) %all-to-all-start.9) | async-done | bytes 2211872 | tf_op jit(solution)/shard_map/all_to_all | solution.py:22
  (120 shorter events, 59.9 us)
Async XLA Ops:
  10.8 35.8 %all-to-all-start = ((bf16[8,3,180,256]{3,2,1,0:T(8,128)(2,1)}), bf16[8,3,180,256]{3,2,1,0:T(8,128)(2,1)}, u32[]{:S(2)}, u32[]{:S(2)}) async-start(bf16[8,3,180,256]{3,2,1,0:T(8,128)(2,1)} %shard_map.94), calls=%async_computation | async-start | bytes 4521984 | tf_op jit(solution)/shard_map/all_to_all | solution.py:22
  18.4 12.5 %copy-start.33 = (f32[768]{0:T(1024)S(1)}, f32[768]{0:T(1024)}, u32[]{:S(2)}) copy-start(f32[768]{0:T(1024)} %param.10) | copy-start | bytes 9220
  20.0 116.7 %copy-start.12 = (s32[4]{0:T(128)}, s32[4]{0:T(128)S(1)}, u32[]{:S(2)}) copy-start(s32[4]{0:T(128)S(1)} %pad_add_fusion.own) | copy-start | bytes 52
  53.5 13.8 %copy-start.20 = (bf16[3,180,256]{2,1,0:T(8,128)(2,1)S(1)}, bf16[3,180,256]{2,1,0:T(8,128)(2,1)}, u32[]{:S(2)}) copy-start(bf16[3,180,256]{2,1,0:T(8,128)(2,1)} %copy-done.19) | copy-start | bytes 829444
  53.5 53.3 %all-to-all-start.1 = ((bf16[256,24,128]{2,1,0:T(8,128)(2,1)}), bf16[256,24,128]{2,1,0:T(8,128)(2,1)}, u32[]{:S(2)}, u32[]{:S(2)}) async-start(bf16[256,24,128]{2,1,0:T(8,128)(2,1)} %shard_map.97), calls=%async_computation.1 | async-start | bytes 3145728 | tf_op jit(solution)/shard_map/all_to_all | solution.py:22
  65.8 70.9 %copy-start = (bf16[16,256,256]{2,1,0:T(8,128)(2,1)S(1)}, bf16[16,256,256]{2,1,0:T(8,128)(2,1)}, u32[]{:S(2)}) copy-start(bf16[16,256,256]{2,1,0:T(8,128)(2,1)} %weight.3) | copy-start | bytes 6291460
  65.9 12.0 %collective-permute-start = (bf16[3,180,256]{2,1,0:T(8,128)(2,1)}, bf16[3,180,256]{2,1,0:T(8,128)(2,1)S(1)}, u32[]{:S(2)}, u32[]{:S(2)}) collective-permute-start(bf16[3,180,256]{2,1,0:T(8,128)(2,1)} %copy-done.21), channel_id=1, source_target_pairs={{0,2},{1,3},{2,0},{3,1},{4,6},{5,7},{6,4},{7,5},{8,10},{9,11},{10,... | collective-permute-start | bytes 829448 | tf_op jit(solution)/shard_map/ppermute | solution.py:537
  67.3 14.2 %collective-permute-start.1 = (bf16[3,180,256]{2,1,0:T(8,128)(2,1)S(1)}, bf16[3,180,256]{2,1,0:T(8,128)(2,1)S(1)}, u32[]{:S(2)}, u32[]{:S(2)}) collective-permute-start(bf16[3,180,256]{2,1,0:T(8,128)(2,1)S(1)} %copy-done.20), channel_id=1, source_target_pairs={{0,6},{1,7},{2,4},{3,5},{4,2},{5,3},{6,0},{7,1},{8,14},{9,15},{10,... | collective-permute-start | bytes 829448 | tf_op jit(solution)/shard_map/ppermute | solution.py:537
  69.1 22.3 %collective-permute-start.2 = (bf16[3,180,256]{2,1,0:T(8,128)(2,1)S(1)}, bf16[3,180,256]{2,1,0:T(8,128)(2,1)}, u32[]{:S(2)}, u32[]{:S(2)}) collective-permute-start(bf16[3,180,256]{2,1,0:T(8,128)(2,1)S(1)} %get-tuple-element.103), channel_id=1, source_target_pairs={{0,4},{1,5},{2,6},{3,7},{4,0},{5,1},{6,2},{7,3},{8,12},{9,13},{10,... | collective-permute-start | bytes 829448 | tf_op jit(solution)/shard_map/ppermute | solution.py:537
  112.7 24.0 %all-to-all-start.2 = ((bf16[32,72,128]{2,1,0:T(8,128)(2,1)}), bf16[32,72,128]{2,1,0:T(8,128)(2,1)S(1)}, u32[]{:S(2)}, u32[]{:S(2)}) async-start(bf16[32,72,128]{2,1,0:T(8,128)(2,1)} %copy-done.8), calls=%async_computation.2 | async-start | bytes 1179648 | tf_op jit(solution)/shard_map/all_to_all | solution.py:22
  117.7 5.0 %collective-permute-start.3 = (bf16[3,180,256]{2,1,0:T(8,128)(2,1)}, bf16[3,180,256]{2,1,0:T(8,128)(2,1)S(1)}, u32[]{:S(2)}, u32[]{:S(2)}) collective-permute-start(bf16[3,180,256]{2,1,0:T(8,128)(2,1)} %copy-done.18), channel_id=1, source_target_pairs={{0,1},{1,0},{2,3},{3,2},{4,5},{5,4},{6,7},{7,6},{8,9},{9,8},{10,11... | collective-permute-start | bytes 829448 | tf_op jit(solution)/shard_map/ppermute | solution.py:537
  119.2 9.6 %collective-permute-start.4 = (bf16[3,180,256]{2,1,0:T(8,128)(2,1)}, bf16[3,180,256]{2,1,0:T(8,128)(2,1)S(1)}, u32[]{:S(2)}, u32[]{:S(2)}) collective-permute-start(bf16[3,180,256]{2,1,0:T(8,128)(2,1)} %copy-done.17), channel_id=1, source_target_pairs={{0,3},{1,2},{2,1},{3,0},{4,7},{5,6},{6,5},{7,4},{8,11},{9,10},{10,... | collective-permute-start | bytes 829448 | tf_op jit(solution)/shard_map/ppermute | solution.py:537
  119.5 16.6 %collective-permute-start.5 = (bf16[3,180,256]{2,1,0:T(8,128)(2,1)}, bf16[3,180,256]{2,1,0:T(8,128)(2,1)S(1)}, u32[]{:S(2)}, u32[]{:S(2)}) collective-permute-start(bf16[3,180,256]{2,1,0:T(8,128)(2,1)} %copy-done.16), channel_id=1, source_target_pairs={{0,7},{1,6},{2,5},{3,4},{4,3},{5,2},{6,1},{7,0},{8,15},{9,14},{10,... | collective-permute-start | bytes 829448 | tf_op jit(solution)/shard_map/ppermute | solution.py:537
  120.5 16.2 %collective-permute-start.6 = (bf16[3,180,256]{2,1,0:T(8,128)(2,1)S(1)}, bf16[3,180,256]{2,1,0:T(8,128)(2,1)}, u32[]{:S(2)}, u32[]{:S(2)}) collective-permute-start(bf16[3,180,256]{2,1,0:T(8,128)(2,1)S(1)} %get-tuple-element.117), channel_id=1, source_target_pairs={{0,5},{1,4},{2,7},{3,6},{4,1},{5,0},{6,3},{7,2},{8,13},{9,12},{10,... | collective-permute-start | bytes 829448 | tf_op jit(solution)/shard_map/ppermute | solution.py:537
  122.7 13.3 %copy-start.25 = (bf16[3,180,256]{2,1,0:T(8,128)(2,1)}, bf16[3,180,256]{2,1,0:T(8,128)(2,1)S(1)}, u32[]{:S(2)}) copy-start(bf16[3,180,256]{2,1,0:T(8,128)(2,1)S(1)} %collective-permute-done.3.refs_1_) | copy-start | bytes 829444
  136.8 28.0 %copy-start.2 = (bf16[2,768,640]{2,1,0:T(8,128)(2,1)S(1)}, bf16[2,768,640]{2,1,0:T(8,128)(2,1)}, u32[]{:S(2)}) copy-start(bf16[2,768,640]{2,1,0:T(8,128)(2,1)} %copy-done.1) | copy-start | bytes 5898244
  229.3 48.8 %all-to-all-start.5 = ((bf16[256,24,128]{2,1,0:T(8,128)(2,1)}), bf16[256,24,128]{2,1,0:T(8,128)(2,1)}, u32[]{:S(2)}, u32[]{:S(2)}) async-start(bf16[256,24,128]{2,1,0:T(8,128)(2,1)} %get-tuple-element.129), calls=%async_computation.5 | async-start | bytes 3145728 | tf_op jit(solution)/shard_map/all_to_all | solution.py:22
  238.4 11.3 %collective-permute-start.7 = (bf16[3,180,256]{2,1,0:T(8,128)(2,1)S(1)}, bf16[3,180,256]{2,1,0:T(8,128)(2,1)S(1)}, u32[]{:S(2)}, u32[]{:S(2)}) collective-permute-start(bf16[3,180,256]{2,1,0:T(8,128)(2,1)S(1)} %get-tuple-element.161), channel_id=1, source_target_pairs={{0,2},{1,3},{2,0},{3,1},{4,6},{5,7},{6,4},{7,5},{8,10},{9,11},{10,... | collective-permute-start | bytes 829448 | tf_op jit(solution)/shard_map/ppermute | solution.py:537
  239.9 22.4 %collective-permute-start.8 = (bf16[3,180,256]{2,1,0:T(8,128)(2,1)S(1)}, bf16[3,180,256]{2,1,0:T(8,128)(2,1)S(1)}, u32[]{:S(2)}, u32[]{:S(2)}) collective-permute-start(bf16[3,180,256]{2,1,0:T(8,128)(2,1)S(1)} %get-tuple-element.160), channel_id=1, source_target_pairs={{0,6},{1,7},{2,4},{3,5},{4,2},{5,3},{6,0},{7,1},{8,14},{9,15},{10,... | collective-permute-start | bytes 829448 | tf_op jit(solution)/shard_map/ppermute | solution.py:537
  241.7 22.6 %collective-permute-start.9 = (bf16[3,180,256]{2,1,0:T(8,128)(2,1)S(1)}, bf16[3,180,256]{2,1,0:T(8,128)(2,1)}, u32[]{:S(2)}, u32[]{:S(2)}) collective-permute-start(bf16[3,180,256]{2,1,0:T(8,128)(2,1)S(1)} %get-tuple-element.159), channel_id=1, source_target_pairs={{0,4},{1,5},{2,6},{3,7},{4,0},{5,1},{6,2},{7,3},{8,12},{9,13},{10,... | collective-permute-start | bytes 829448 | tf_op jit(solution)/shard_map/ppermute | solution.py:537
  249.7 34.1 %copy-start.28 = (bf16[3,180,256]{2,1,0:T(8,128)(2,1)}, bf16[3,180,256]{2,1,0:T(8,128)(2,1)S(1)}, u32[]{:S(2)}) copy-start(bf16[3,180,256]{2,1,0:T(8,128)(2,1)S(1)} %collective-permute-done.7.refs_2_) | copy-start | bytes 829444
  283.8 25.6 %copy-start.13 = (s32[4]{0:T(128)S(1)}, s32[4]{0:T(128)}, u32[]{:S(2)}) copy-start(s32[4]{0:T(128)} %copy-done.12) | copy-start | bytes 52
  283.8 25.5 %all-to-all-start.6 = ((bf16[32,72,128]{2,1,0:T(8,128)(2,1)}), bf16[32,72,128]{2,1,0:T(8,128)(2,1)}, u32[]{:S(2)}, u32[]{:S(2)}) async-start(bf16[32,72,128]{2,1,0:T(8,128)(2,1)} %copy-done.7), calls=%async_computation.6 | async-start | bytes 1179648 | tf_op jit(solution)/shard_map/all_to_all | solution.py:22
  290.4 5.0 %collective-permute-start.10 = (bf16[3,180,256]{2,1,0:T(8,128)(2,1)S(1)}, bf16[3,180,256]{2,1,0:T(8,128)(2,1)S(1)}, u32[]{:S(2)}, u32[]{:S(2)}) collective-permute-start(bf16[3,180,256]{2,1,0:T(8,128)(2,1)S(1)} %get-tuple-element.158), channel_id=1, source_target_pairs={{0,1},{1,0},{2,3},{3,2},{4,5},{5,4},{6,7},{7,6},{8,9},{9,8},{10,11... | collective-permute-start | bytes 829448 | tf_op jit(solution)/shard_map/ppermute | solution.py:537
  291.8 9.4 %collective-permute-start.11 = (bf16[3,180,256]{2,1,0:T(8,128)(2,1)S(1)}, bf16[3,180,256]{2,1,0:T(8,128)(2,1)S(1)}, u32[]{:S(2)}, u32[]{:S(2)}) collective-permute-start(bf16[3,180,256]{2,1,0:T(8,128)(2,1)S(1)} %get-tuple-element.157), channel_id=1, source_target_pairs={{0,3},{1,2},{2,1},{3,0},{4,7},{5,6},{6,5},{7,4},{8,11},{9,10},{10,... | collective-permute-start | bytes 829448 | tf_op jit(solution)/shard_map/ppermute | solution.py:537
  292.1 16.5 %collective-permute-start.12 = (bf16[3,180,256]{2,1,0:T(8,128)(2,1)S(1)}, bf16[3,180,256]{2,1,0:T(8,128)(2,1)S(1)}, u32[]{:S(2)}, u32[]{:S(2)}) collective-permute-start(bf16[3,180,256]{2,1,0:T(8,128)(2,1)S(1)} %get-tuple-element.156), channel_id=1, source_target_pairs={{0,7},{1,6},{2,5},{3,4},{4,3},{5,2},{6,1},{7,0},{8,15},{9,14},{10,... | collective-permute-start | bytes 829448 | tf_op jit(solution)/shard_map/ppermute | solution.py:537
  293.8 15.5 %collective-permute-start.13 = (bf16[3,180,256]{2,1,0:T(8,128)(2,1)S(1)}, bf16[3,180,256]{2,1,0:T(8,128)(2,1)}, u32[]{:S(2)}, u32[]{:S(2)}) collective-permute-start(bf16[3,180,256]{2,1,0:T(8,128)(2,1)S(1)} %get-tuple-element.155), channel_id=1, source_target_pairs={{0,5},{1,4},{2,7},{3,6},{4,1},{5,0},{6,3},{7,2},{8,13},{9,12},{10,... | collective-permute-start | bytes 829448 | tf_op jit(solution)/shard_map/ppermute | solution.py:537
  295.4 48.7 %copy-start.30 = (bf16[3,180,256]{2,1,0:T(8,128)(2,1)}, bf16[3,180,256]{2,1,0:T(8,128)(2,1)S(1)}, u32[]{:S(2)}) copy-start(bf16[3,180,256]{2,1,0:T(8,128)(2,1)S(1)} %collective-permute-done.10.refs_1_) | copy-start | bytes 829444
  309.3 31.8 %copy-start.3 = (bf16[2,768,640]{2,1,0:T(8,128)(2,1)S(1)}, bf16[2,768,640]{2,1,0:T(8,128)(2,1)}, u32[]{:S(2)}) copy-start(bf16[2,768,640]{2,1,0:T(8,128)(2,1)} %copy-done.1) | copy-start | bytes 5898244
  344.1 49.3 %all-to-all-start.8 = ((bf16[256,24,128]{2,1,0:T(8,128)(2,1)}), bf16[256,24,128]{2,1,0:T(8,128)(2,1)S(1)}, u32[]{:S(2)}, u32[]{:S(2)}) async-start(bf16[256,24,128]{2,1,0:T(8,128)(2,1)} %shard_map.104), calls=%async_computation.8 | async-start | bytes 3145728 | tf_op jit(solution)/shard_map/all_to_all | solution.py:22
  351.7 55.6 %reduce-scatter.2.cloned.1.call-start = ((), (), s32[]{:S(2)}) async-start(), calls=%async_computation.11 | async-start | bytes 2359296 | tf_op jit(solution)/shard_map/reduce_scatter | solution.py:728
  401.9 33.5 %all-to-all-start.9 = ((bf16[8,3,180,256]{3,2,1,0:T(8,128)(2,1)}), bf16[8,3,180,256]{3,2,1,0:T(8,128)(2,1)S(1)}, u32[]{:S(2)}, u32[]{:S(2)}) async-start(bf16[8,3,180,256]{3,2,1,0:T(8,128)(2,1)} %shard_map.105), calls=%async_computation.9 | async-start | bytes 4521984 | tf_op jit(solution)/shard_map/all_to_all | solution.py:22
  (24 other events, 78.2 us)
Sparse Core Ops, SparseCore 0:
  355.6 38.5 reduce-scatter.1
where the time goes:
time: 453 us; the launch traced here: 445 us
  waiting for transfers between devices  170 us (38%)
  blocking collectives  104 us (23%)
  starting transfers between devices  69.4 us (15%)
  Pallas kernels  57.1 us (13%)
  local copies, waits for them, and re-layouts  21 us (5%)
  between operations  14.9 us (3%)
  other arithmetic  7.86 us (2%)
    all_to_all x3, blocking collectives, exchange(): lax.all_to_all(payload, axes, split_axis=0, concat_axis=0, tiled=True)  104 us
    all_to_all x7, waiting for transfers between devices, exchange(): lax.all_to_all(payload, axes, split_axis=0, concat_axis=0, tiled=True)  101 us
    ppermute x14, waiting for transfers between devices, beside(): moved = [lax.ppermute(piece(bands, k), 'azimuth', trade[k]) for k in kinds]  68.5 us
    all_to_all x7, starting transfers between devices, exchange(): lax.all_to_all(payload, axes, split_axis=0, concat_axis=0, tiled=True)  51.1 us
    pallas_call x11, Pallas kernels, kernel_call(): pl.pallas_call(kernel, out_shape=outs, in_specs=in_specs, out_specs=out_s...  49.7 us
    ppermute x14, starting transfers between devices, beside(): moved = [lax.ppermute(piece(bands, k), 'azimuth', trade[k]) for k in kinds]  17.9 us
    unnamed x69, local copies, waits for them, and re-layouts  13.8 us
  transfers between devices with their start and end apart: 22, of which 15 were waited for; matrix products, arithmetic and copies ran while one was open for 3% of the time, Pallas kernels for 4%

commit v1 on v0

--- a/solution.py
+++ b/solution.py
@@ -14,6 +14,8 @@
 ROW_PAD = 192
 MIB = 1024 * 1024
 WHOLE = 56
+APART = 56
+PIECES = 4
 GELU_A = math.sqrt(2.0 / math.pi)
 GELU_B = 0.044715
 
@@ -72,8 +74,15 @@
 
 
 def analysis_kernel(weighted, received, lat_w, folded_far, out, wide, columns, folded, arrival):
-    fetch = pltpu.make_async_copy(folded_far, folded, arrival)
-    fetch.start()
+    size = folded.shape[0] // PIECES
+    fetches = [
+        pltpu.make_async_copy(
+            folded_far.at[pl.ds(c * size, size)], folded.at[pl.ds(c * size, size)], arrival.at[c]
+        )
+        for c in range(PIECES)
+    ]
+    for fetch in fetches:
+        fetch.start()
     peers = received.shape[0]
     wide[...] = received[...].astype(F32).reshape(wide.shape)
     rows = received.shape[1] // 8
@@ -89,7 +98,8 @@
                         block = block * lat_w[row * peers : (row + 1) * peers, :]
                     lane = (part * 2 + half) * LANES
                     columns[start : start + peers, lane : lane + LANES] = block.astype(BF16)
-    fetch.wait()
+    for fetch in fetches:
+        fetch.wait()
     total = jnp.dot(folded[...], columns[...], preferred_element_type=F32).astype(BF16)
     groups = out.shape[0]
     for quarter in range(4):
@@ -447,7 +457,7 @@
             ordered[...], chosen[slot], turned, preferred_element_type=F32
         ).astype(BF16)
         folded[:, slot * lat_all : (slot + 1) * lat_all] = lax.dot_general(
-            chosen[slot, : degree_count + 16, :], ordered[...], turned, preferred_element_type=F32
+            chosen[slot, : folded.shape[0], :], ordered[...], turned, preferred_element_type=F32
         ).astype(BF16)
 
 
@@ -540,7 +550,7 @@
         done.update(zip(kinds, moved))
         return payload, bands
 
-    groups = ((2, 6, 4), (1, 3, 7, 5))
+    groups = ((2, 6, 4, 5), (1, 3, 7))
 
     turned_field = jnp.transpose(field, (1, 0, 2))
     grid = exchange(
@@ -558,7 +568,7 @@
     folded, spread = kernel_call(
         degree_tables_kernel,
         (
-            jax.ShapeDtypeStruct((degree_count + 16, slots * lat_all), BF16),
+            jax.ShapeDtypeStruct((degree_count + LANES // 2, slots * lat_all), BF16),
             jax.ShapeDtypeStruct((slots, lat_all, degree_count + LANES), BF16),
         ),
         [smem, smem, smem, vmem],
@@ -622,9 +632,9 @@
                 wide,
                 pltpu.VMEM((slots * lat_all, 4 * LANES), BF16),
                 pltpu.VMEM(folded.shape, BF16),
-                sems,
+                sems((PIECES,)),
             ],
-            24,
+            APART,
             800_000_000,
             received,
             lat_w,
@@ -651,7 +661,7 @@
         [vmem, vmem],
         vmem,
         [wide, held_table, stages],
-        WHOLE,
+        24,
         2_400_000_000,
         grid,
         table_back,

time: 453 us -> 442 us (0.976)
  blocking collectives: 104 us -> 94.1 us
  starting transfers between devices: 69.4 us -> 75.1 us
    all_to_all x7, waiting for transfers between devices: 101 us -> 89.8 us  [exchange(): lax.all_to_all(payload, axes, split_axis=0, concat_axis=0, tiled=True)]
    all_to_all x3, blocking collectives: 104 us -> 94.1 us  [exchange(): lax.all_to_all(payload, axes, split_axis=0, concat_axis=0, tiled=True)]
    ppermute x14, waiting for transfers between devices: 68.5 us -> 75.5 us  [beside(): moved = [lax.ppermute(piece(bands, k), 'azimuth', trade[k]) for k in kinds]]
    all_to_all x7, starting transfers between devices: 51.1 us -> 56 us  [exchange(): lax.all_to_all(payload, axes, split_axis=0, concat_axis=0, tiled=True)]
  transfers between devices with their start and end apart: 22 -> 22, of which waited for: 15 -> 18; matrix products, arithmetic and copies ran while one was open for 3% -> 3% of each run, Pallas kernels for 4% -> 4%
where the time goes in v1:
time: 442 us; the launch traced here: 433 us
  waiting for transfers between devices  166 us (38%)
  blocking collectives  94.1 us (21%)
  starting transfers between devices  75.1 us (17%)
  Pallas kernels  57.4 us (13%)
  local copies, waits for them, and re-layouts  19.2 us (4%)
  between operations  14.9 us (3%)
  other arithmetic  6.48 us (1%)
    all_to_all x3, blocking collectives, exchange(): lax.all_to_all(payload, axes, split_axis=0, concat_axis=0, tiled=True)  94.1 us
    all_to_all x7, waiting for transfers between devices, exchange(): lax.all_to_all(payload, axes, split_axis=0, concat_axis=0, tiled=True)  89.8 us
    ppermute x14, waiting for transfers between devices, beside(): moved = [lax.ppermute(piece(bands, k), 'azimuth', trade[k]) for k in kinds]  75.5 us
    all_to_all x7, starting transfers between devices, exchange(): lax.all_to_all(payload, axes, split_axis=0, concat_axis=0, tiled=True)  56 us
    pallas_call x11, Pallas kernels, kernel_call(): pl.pallas_call(kernel, out_shape=outs, in_specs=in_specs, out_specs=out_s...  50 us
    ppermute x14, starting transfers between devices, beside(): moved = [lax.ppermute(piece(bands, k), 'azimuth', trade[k]) for k in kinds]  19 us
    unnamed x69, local copies, waits for them, and re-layouts  11.3 us
  transfers between devices with their start and end apart: 22, of which 18 were waited for; matrix products, arithmetic and copies ran while one was open for 3% of the time, Pallas kernels for 4%

profile of v1, /device:TPU:1, one launch (start us, length us, event | category | flops | bytes accessed | tf_op | source)
XLA Modules:
  0.0 433.0 jit_solution(9197389042875670878)
XLA Ops:
  7.2 3.6 shard_map.94
  10.8 7.6 %all-to-all-start = ((bf16[8,3,180,256]{3,2,1,0:T(8,128)(2,1)}), bf16[8,3,180,256]{3,2,1,0:T(8,128)(2,1)}, u32[]{:S(2)}, u32[]{:S(2)}) async-start(bf16[8,3,180,256]{3,2,1,0:T(8,128)(2,1)} %shard_map.94), calls=%async_computation | async-start | bytes 4521984 | tf_op jit(solution)/shard_map/all_to_all | solution.py:24
  36.3 10.3 %all-to-all-done.grid.grid_far = bf16[8,3,180,256]{3,2,1,0:T(8,128)(2,1)} async-done(((bf16[8,3,180,256]{3,2,1,0:T(8,128)(2,1)}), bf16[8,3,180,256]{3,2,1,0:T(8,128)(2,1)}, u32[]{:S(2)}, u32[]{:S(2)}) %all-to-all-start) | async-done | bytes 2211872 | tf_op jit(solution)/shard_map/all_to_all | solution.py:24
  47.5 4.6 %shard_map.97 = bf16[256,24,128]{2,1,0:T(8,128)(2,1)S(1)} custom-call(bf16[8,3,180,256]{3,2,1,0:T(8,128)(2,1)} %all-to-all-done.grid.grid_far, bf16[1536,1024]{1,0:T(8,128)(2,1)S(1)} %bitcast.33), custom_call_target="tpu_custom_call" | custom-call | flops 2400000000 | bytes 2400000 | tf_op jit(solution)/shard_map/pallas_call | solution.py:508
  53.3 12.4 %all-to-all-start.1 = ((bf16[256,24,128]{2,1,0:T(8,128)(2,1)}), bf16[256,24,128]{2,1,0:T(8,128)(2,1)}, u32[]{:S(2)}, u32[]{:S(2)}) async-start(bf16[256,24,128]{2,1,0:T(8,128)(2,1)} %copy-done.9), calls=%async_computation.1 | async-start | bytes 3145728 | tf_op jit(solution)/shard_map/all_to_all | solution.py:24
  73.0 4.7 %collective-permute-done.refs_2_ = bf16[3,180,256]{2,1,0:T(8,128)(2,1)S(1)} collective-permute-done((bf16[3,180,256]{2,1,0:T(8,128)(2,1)}, bf16[3,180,256]{2,1,0:T(8,128)(2,1)S(1)}, u32[]{:S(2)}, u32[]{:S(2)}) %collective-permute-start) | collective-permute-done | bytes 276512 | tf_op jit(solution)/shard_map/ppermute | solution.py:547
  77.7 22.4 %collective-permute-done.1.refs_6_ = bf16[3,180,256]{2,1,0:T(8,128)(2,1)S(1)} collective-permute-done((bf16[3,180,256]{2,1,0:T(8,128)(2,1)}, bf16[3,180,256]{2,1,0:T(8,128)(2,1)S(1)}, u32[]{:S(2)}, u32[]{:S(2)}) %collective-permute-start.1) | collective-permute-done | bytes 276512 | tf_op jit(solution)/shard_map/ppermute | solution.py:547
  102.9 3.7 all-to-all-done.1.received
  106.6 4.9 %shard_map.98 = bf16[32,72,128]{2,1,0:T(8,128)(2,1)} custom-call(bf16[256,24,128]{2,1,0:T(8,128)(2,1)} %all-to-all-done.1.received, f32[768,128]{1,0:T(8,128)} %broadcast_in_dim.28.lat_w, bf16[576,1536]{1,0:T(8,128)(2,1)} %copy-done.7), custom_call_target="tpu_custom_call" | custom-call | flops 800000000 | bytes 800000 | tf_op jit(solution)/shard_map/pallas_call | solution.py:508
  111.5 6.0 %all-to-all-start.2 = ((bf16[32,72,128]{2,1,0:T(8,128)(2,1)}), bf16[32,72,128]{2,1,0:T(8,128)(2,1)S(1)}, u32[]{:S(2)}, u32[]{:S(2)}) async-start(bf16[32,72,128]{2,1,0:T(8,128)(2,1)} %shard_map.98), calls=%async_computation.2 | async-start | bytes 1179648 | tf_op jit(solution)/shard_map/all_to_all | solution.py:24
  119.8 7.6 %collective-permute-done.5.refs_3_ = bf16[3,180,256]{2,1,0:T(8,128)(2,1)S(1)} collective-permute-done((bf16[3,180,256]{2,1,0:T(8,128)(2,1)}, bf16[3,180,256]{2,1,0:T(8,128)(2,1)S(1)}, u32[]{:S(2)}, u32[]{:S(2)}) %collective-permute-start.5) | collective-permute-done | bytes 276512 | tf_op jit(solution)/shard_map/ppermute | solution.py:547
  128.7 6.4 %all-to-all-done.2.received.coeffs = bf16[32,72,128]{2,1,0:T(8,128)(2,1)S(1)} async-done(((bf16[32,72,128]{2,1,0:T(8,128)(2,1)}), bf16[32,72,128]{2,1,0:T(8,128)(2,1)S(1)}, u32[]{:S(2)}, u32[]{:S(2)}) %all-to-all-start.2) | async-done | bytes 589856 | tf_op jit(solution)/shard_map/all_to_all | solution.py:24
  136.5 21.7 %all_to_all.50.received = bf16[32,72,128]{2,1,0:T(8,128)(2,1)S(1)} all-to-all(bf16[32,72,128]{2,1,0:T(8,128)(2,1)S(1)} %shard_map.99), channel_id=1, replica_groups=mesh['polar'=32,'azimuth'=8] {'polar'}, dimensions={0} | all-to-all | bytes 1179648 | tf_op jit(solution)/shard_map/all_to_all | solution.py:24
  159.7 50.9 %all_to_all.51.received = bf16[256,24,128]{2,1,0:T(8,128)(2,1)} all-to-all(bf16[256,24,128]{2,1,0:T(8,128)(2,1)S(1)} %shard_map.100), channel_id=1, replica_groups=mesh['polar'=32,'azimuth'=8] {'polar','azimuth'}, dimensions={0} | all-to-all | bytes 3145728 | tf_op jit(solution)/shard_map/all_to_all | solution.py:24
  210.6 13.0 %shard_map.101 = (bf16[256,24,128]{2,1,0:T(8,128)(2,1)}, bf16[8,3,180,256]{3,2,1,0:T(8,128)(2,1)}) custom-call(s32[4]{0:T(128)} %copy-done.12, bf16[256,24,128]{2,1,0:T(8,128)(2,1)} %all_to_all.51.received, bf16[1536,1024]{1,0:T(8,128)(2,1)} %bitcast.34, bf16[8,3,180,256]{3,2,1,0:T(8,128)(2,1)} %all-to-all-done.grid.grid_far, ...), custom_call_target="tpu_custom_call" | custom-call | flops 4800000000 | bytes 4800000 | tf_op jit(solution)/shard_map/pallas_call | solution.py:508
  223.6 8.1 %all-to-all-start.5 = ((bf16[256,24,128]{2,1,0:T(8,128)(2,1)}), bf16[256,24,128]{2,1,0:T(8,128)(2,1)}, u32[]{:S(2)}, u32[]{:S(2)}) async-start(bf16[256,24,128]{2,1,0:T(8,128)(2,1)} %get-tuple-element.125), calls=%async_computation.5 | async-start | bytes 3145728 | tf_op jit(solution)/shard_map/all_to_all | solution.py:24
  239.8 7.5 %collective-permute-done.10.refs_5_ = bf16[3,180,256]{2,1,0:T(8,128)(2,1)S(1)} collective-permute-done((bf16[3,180,256]{2,1,0:T(8,128)(2,1)S(1)}, bf16[3,180,256]{2,1,0:T(8,128)(2,1)S(1)}, u32[]{:S(2)}, u32[]{:S(2)}) %collective-permute-start.10) | collective-permute-done | bytes 276512 | tf_op jit(solution)/shard_map/ppermute | solution.py:547
  247.2 12.1 %collective-permute-done.7.refs_2_ = bf16[3,180,256]{2,1,0:T(8,128)(2,1)S(1)} collective-permute-done((bf16[3,180,256]{2,1,0:T(8,128)(2,1)S(1)}, bf16[3,180,256]{2,1,0:T(8,128)(2,1)S(1)}, u32[]{:S(2)}, u32[]{:S(2)}) %collective-permute-start.7) | collective-permute-done | bytes 276512 | tf_op jit(solution)/shard_map/ppermute | solution.py:547
  259.3 3.8 collective-permute-done.8.refs_6_
  263.8 5.9 %collective-permute-done.9.refs_4_ = bf16[3,180,256]{2,1,0:T(8,128)(2,1)} collective-permute-done((bf16[3,180,256]{2,1,0:T(8,128)(2,1)S(1)}, bf16[3,180,256]{2,1,0:T(8,128)(2,1)}, u32[]{:S(2)}, u32[]{:S(2)}) %collective-permute-start.9) | collective-permute-done | bytes 276512 | tf_op jit(solution)/shard_map/ppermute | solution.py:547
  272.6 4.8 %shard_map.102 = bf16[32,72,128]{2,1,0:T(8,128)(2,1)} custom-call(bf16[256,24,128]{2,1,0:T(8,128)(2,1)} %all-to-all-done.5.received, f32[768,128]{1,0:T(8,128)} %broadcast_in_dim.28.lat_w, bf16[576,1536]{1,0:T(8,128)(2,1)} %copy-done.7), custom_call_target="tpu_custom_call" | custom-call | flops 800000000 | bytes 800000 | tf_op jit(solution)/shard_map/pallas_call | solution.py:508
  277.4 6.7 %all-to-all-start.6 = ((bf16[32,72,128]{2,1,0:T(8,128)(2,1)}), bf16[32,72,128]{2,1,0:T(8,128)(2,1)}, u32[]{:S(2)}, u32[]{:S(2)}) async-start(bf16[32,72,128]{2,1,0:T(8,128)(2,1)} %shard_map.102), calls=%async_computation.6 | async-start | bytes 1179648 | tf_op jit(solution)/shard_map/all_to_all | solution.py:24
  288.1 7.0 %collective-permute-done.12.refs_3_ = bf16[3,180,256]{2,1,0:T(8,128)(2,1)S(1)} collective-permute-done((bf16[3,180,256]{2,1,0:T(8,128)(2,1)S(1)}, bf16[3,180,256]{2,1,0:T(8,128)(2,1)S(1)}, u32[]{:S(2)}, u32[]{:S(2)}) %collective-permute-start.12) | collective-permute-done | bytes 276512 | tf_op jit(solution)/shard_map/ppermute | solution.py:547
  297.0 4.7 %all-to-all-done.6.received = bf16[32,72,128]{2,1,0:T(8,128)(2,1)} async-done(((bf16[32,72,128]{2,1,0:T(8,128)(2,1)}), bf16[32,72,128]{2,1,0:T(8,128)(2,1)}, u32[]{:S(2)}, u32[]{:S(2)}) %all-to-all-start.6) | async-done | bytes 589856 | tf_op jit(solution)/shard_map/all_to_all | solution.py:24
  301.7 4.3 shard_map.103
  306.0 21.6 %all_to_all.52.received = bf16[32,72,128]{2,1,0:T(8,128)(2,1)S(1)} all-to-all(bf16[32,72,128]{2,1,0:T(8,128)(2,1)S(1)} %get-tuple-element.132), channel_id=1, replica_groups=mesh['polar'=32,'azimuth'=8] {'polar'}, dimensions={0} | all-to-all | bytes 1179648 | tf_op jit(solution)/shard_map/all_to_all | solution.py:24
  330.4 9.9 %all-to-all-start.8 = ((bf16[256,24,128]{2,1,0:T(8,128)(2,1)}), bf16[256,24,128]{2,1,0:T(8,128)(2,1)S(1)}, u32[]{:S(2)}, u32[]{:S(2)}) async-start(bf16[256,24,128]{2,1,0:T(8,128)(2,1)} %shard_map.104), calls=%async_computation.8 | async-start | bytes 3145728 | tf_op jit(solution)/shard_map/all_to_all | solution.py:24
  342.7 39.3 %all-to-all-done.8.received = bf16[256,24,128]{2,1,0:T(8,128)(2,1)S(1)} async-done(((bf16[256,24,128]{2,1,0:T(8,128)(2,1)}), bf16[256,24,128]{2,1,0:T(8,128)(2,1)S(1)}, u32[]{:S(2)}, u32[]{:S(2)}) %all-to-all-start.8) | async-done | bytes 1572896 | tf_op jit(solution)/shard_map/all_to_all | solution.py:24
  383.1 7.4 %shard_map.105 = bf16[8,3,180,256]{3,2,1,0:T(8,128)(2,1)} custom-call(s32[4]{0:T(128)} %copy-done.12, bf16[256,24,128]{2,1,0:T(8,128)(2,1)} %copy-done.22, bf16[1536,1024]{1,0:T(8,128)(2,1)} %bitcast.35, bf16[3,180,256]{2,1,0:T(8,128)(2,1)} %copy-done.11, bf16[3,180,256]{2,1,0:T(8,128)(2,1)} %copy-done.26, bf16[3,180,256]{2,1,0:T(8,128)(2,1)} %copy-done.23, ...), custom_call_target="tpu_custom_call" | custom-call | flops 2400000000 | bytes 2400000 | tf_op jit(solution)/shard_map/pallas_call | solution.py:508
  390.5 5.4 %all-to-all-start.9 = ((bf16[8,3,180,256]{3,2,1,0:T(8,128)(2,1)}), bf16[8,3,180,256]{3,2,1,0:T(8,128)(2,1)S(1)}, u32[]{:S(2)}, u32[]{:S(2)}) async-start(bf16[8,3,180,256]{3,2,1,0:T(8,128)(2,1)} %shard_map.105), calls=%async_computation.9 | async-start | bytes 4521984 | tf_op jit(solution)/shard_map/all_to_all | solution.py:24
  397.7 3.8 shard_map.106
  401.5 22.5 %all-to-all-done.9 = bf16[8,3,180,256]{3,2,1,0:T(8,128)(2,1)S(1)} async-done(((bf16[8,3,180,256]{3,2,1,0:T(8,128)(2,1)}), bf16[8,3,180,256]{3,2,1,0:T(8,128)(2,1)S(1)}, u32[]{:S(2)}, u32[]{:S(2)}) %all-to-all-start.9) | async-done | bytes 2211872 | tf_op jit(solution)/shard_map/all_to_all | solution.py:24
  (120 shorter events, 64.0 us)
Async XLA Ops:
  10.8 35.8 %all-to-all-start = ((bf16[8,3,180,256]{3,2,1,0:T(8,128)(2,1)}), bf16[8,3,180,256]{3,2,1,0:T(8,128)(2,1)}, u32[]{:S(2)}, u32[]{:S(2)}) async-start(bf16[8,3,180,256]{3,2,1,0:T(8,128)(2,1)} %shard_map.94), calls=%async_computation | async-start | bytes 4521984 | tf_op jit(solution)/shard_map/all_to_all | solution.py:24
  20.0 115.1 %copy-start.12 = (s32[4]{0:T(128)}, s32[4]{0:T(128)S(1)}, u32[]{:S(2)}) copy-start(s32[4]{0:T(128)S(1)} %pad_add_fusion.own) | copy-start | bytes 52
  53.3 53.3 %all-to-all-start.1 = ((bf16[256,24,128]{2,1,0:T(8,128)(2,1)}), bf16[256,24,128]{2,1,0:T(8,128)(2,1)}, u32[]{:S(2)}, u32[]{:S(2)}) async-start(bf16[256,24,128]{2,1,0:T(8,128)(2,1)} %copy-done.9), calls=%async_computation.1 | async-start | bytes 3145728 | tf_op jit(solution)/shard_map/all_to_all | solution.py:24
  65.7 69.4 %copy-start.3 = (bf16[16,256,256]{2,1,0:T(8,128)(2,1)S(1)}, bf16[16,256,256]{2,1,0:T(8,128)(2,1)}, u32[]{:S(2)}) copy-start(bf16[16,256,256]{2,1,0:T(8,128)(2,1)} %weight.3) | copy-start | bytes 6291460
  65.7 12.0 %collective-permute-start = (bf16[3,180,256]{2,1,0:T(8,128)(2,1)}, bf16[3,180,256]{2,1,0:T(8,128)(2,1)S(1)}, u32[]{:S(2)}, u32[]{:S(2)}) collective-permute-start(bf16[3,180,256]{2,1,0:T(8,128)(2,1)} %copy-done.21), channel_id=1, source_target_pairs={{0,2},{1,3},{2,0},{3,1},{4,6},{5,7},{6,4},{7,5},{8,10},{9,11},{10,... | collective-permute-start | bytes 829448 | tf_op jit(solution)/shard_map/ppermute | solution.py:547
  67.2 32.9 %collective-permute-start.1 = (bf16[3,180,256]{2,1,0:T(8,128)(2,1)}, bf16[3,180,256]{2,1,0:T(8,128)(2,1)S(1)}, u32[]{:S(2)}, u32[]{:S(2)}) collective-permute-start(bf16[3,180,256]{2,1,0:T(8,128)(2,1)} %copy-done.20), channel_id=1, source_target_pairs={{0,6},{1,7},{2,4},{3,5},{4,2},{5,3},{6,0},{7,1},{8,14},{9,15},{10,... | collective-permute-start | bytes 829448 | tf_op jit(solution)/shard_map/ppermute | solution.py:547
  69.0 31.1 %collective-permute-start.2 = (bf16[3,180,256]{2,1,0:T(8,128)(2,1)}, bf16[3,180,256]{2,1,0:T(8,128)(2,1)S(1)}, u32[]{:S(2)}, u32[]{:S(2)}) collective-permute-start(bf16[3,180,256]{2,1,0:T(8,128)(2,1)} %copy-done.19), channel_id=1, source_target_pairs={{0,4},{1,5},{2,6},{3,7},{4,0},{5,1},{6,2},{7,3},{8,12},{9,13},{10,... | collective-permute-start | bytes 829448 | tf_op jit(solution)/shard_map/ppermute | solution.py:547
  69.6 33.4 %collective-permute-start.3 = (bf16[3,180,256]{2,1,0:T(8,128)(2,1)}, bf16[3,180,256]{2,1,0:T(8,128)(2,1)}, u32[]{:S(2)}, u32[]{:S(2)}) collective-permute-start(bf16[3,180,256]{2,1,0:T(8,128)(2,1)} %copy-done.18), channel_id=1, source_target_pairs={{0,5},{1,4},{2,7},{3,6},{4,1},{5,0},{6,3},{7,2},{8,13},{9,12},{10,... | collective-permute-start | bytes 829448 | tf_op jit(solution)/shard_map/ppermute | solution.py:547
  77.7 33.8 %copy-start.23 = (bf16[3,180,256]{2,1,0:T(8,128)(2,1)}, bf16[3,180,256]{2,1,0:T(8,128)(2,1)S(1)}, u32[]{:S(2)}) copy-start(bf16[3,180,256]{2,1,0:T(8,128)(2,1)S(1)} %collective-permute-done.refs_2_) | copy-start | bytes 829444
  111.5 23.6 %all-to-all-start.2 = ((bf16[32,72,128]{2,1,0:T(8,128)(2,1)}), bf16[32,72,128]{2,1,0:T(8,128)(2,1)S(1)}, u32[]{:S(2)}, u32[]{:S(2)}) async-start(bf16[32,72,128]{2,1,0:T(8,128)(2,1)} %shard_map.98), calls=%async_computation.2 | async-start | bytes 1179648 | tf_op jit(solution)/shard_map/all_to_all | solution.py:24
  117.5 40.6 %copy-start.1 = (f32[768,128]{1,0:T(8,128)S(1)}, f32[768,128]{1,0:T(8,128)}, u32[]{:S(2)}) copy-start(f32[768,128]{1,0:T(8,128)} %broadcast_in_dim.28.lat_w) | copy-start | bytes 1179652
  117.6 2.3 collective-permute-start.4
  118.4 9.1 %collective-permute-start.5 = (bf16[3,180,256]{2,1,0:T(8,128)(2,1)}, bf16[3,180,256]{2,1,0:T(8,128)(2,1)S(1)}, u32[]{:S(2)}, u32[]{:S(2)}) collective-permute-start(bf16[3,180,256]{2,1,0:T(8,128)(2,1)} %copy-done.16), channel_id=1, source_target_pairs={{0,3},{1,2},{2,1},{3,0},{4,7},{5,6},{6,5},{7,4},{8,11},{9,10},{10,... | collective-permute-start | bytes 829448 | tf_op jit(solution)/shard_map/ppermute | solution.py:547
  118.4 10.3 %collective-permute-start.6 = (bf16[3,180,256]{2,1,0:T(8,128)(2,1)S(1)}, bf16[3,180,256]{2,1,0:T(8,128)(2,1)}, u32[]{:S(2)}, u32[]{:S(2)}) collective-permute-start(bf16[3,180,256]{2,1,0:T(8,128)(2,1)S(1)} %get-tuple-element.114), channel_id=1, source_target_pairs={{0,7},{1,6},{2,5},{3,4},{4,3},{5,2},{6,1},{7,0},{8,15},{9,14},{10,... | collective-permute-start | bytes 829448 | tf_op jit(solution)/shard_map/ppermute | solution.py:547
  135.1 23.0 %copy-start.5 = (bf16[2,768,640]{2,1,0:T(8,128)(2,1)S(1)}, bf16[2,768,640]{2,1,0:T(8,128)(2,1)}, u32[]{:S(2)}) copy-start(bf16[2,768,640]{2,1,0:T(8,128)(2,1)} %copy-done.4) | copy-start | bytes 5898244
  223.6 49.0 %all-to-all-start.5 = ((bf16[256,24,128]{2,1,0:T(8,128)(2,1)}), bf16[256,24,128]{2,1,0:T(8,128)(2,1)}, u32[]{:S(2)}, u32[]{:S(2)}) async-start(bf16[256,24,128]{2,1,0:T(8,128)(2,1)} %get-tuple-element.125), calls=%async_computation.5 | async-start | bytes 3145728 | tf_op jit(solution)/shard_map/all_to_all | solution.py:24
  233.0 14.2 %collective-permute-start.10 = (bf16[3,180,256]{2,1,0:T(8,128)(2,1)S(1)}, bf16[3,180,256]{2,1,0:T(8,128)(2,1)S(1)}, u32[]{:S(2)}, u32[]{:S(2)}) collective-permute-start(bf16[3,180,256]{2,1,0:T(8,128)(2,1)S(1)} %get-tuple-element.154), channel_id=1, source_target_pairs={{0,5},{1,4},{2,7},{3,6},{4,1},{5,0},{6,3},{7,2},{8,13},{9,12},{10,... | collective-permute-start | bytes 829448 | tf_op jit(solution)/shard_map/ppermute | solution.py:547
  236.3 23.0 %collective-permute-start.7 = (bf16[3,180,256]{2,1,0:T(8,128)(2,1)S(1)}, bf16[3,180,256]{2,1,0:T(8,128)(2,1)S(1)}, u32[]{:S(2)}, u32[]{:S(2)}) collective-permute-start(bf16[3,180,256]{2,1,0:T(8,128)(2,1)S(1)} %get-tuple-element.157), channel_id=1, source_target_pairs={{0,2},{1,3},{2,0},{3,1},{4,6},{5,7},{6,4},{7,5},{8,10},{9,11},{10,... | collective-permute-start | bytes 829448 | tf_op jit(solution)/shard_map/ppermute | solution.py:547
  236.6 26.5 %collective-permute-start.8 = (bf16[3,180,256]{2,1,0:T(8,128)(2,1)S(1)}, bf16[3,180,256]{2,1,0:T(8,128)(2,1)S(1)}, u32[]{:S(2)}, u32[]{:S(2)}) collective-permute-start(bf16[3,180,256]{2,1,0:T(8,128)(2,1)S(1)} %get-tuple-element.156), channel_id=1, source_target_pairs={{0,6},{1,7},{2,4},{3,5},{4,2},{5,3},{6,0},{7,1},{8,14},{9,15},{10,... | collective-permute-start | bytes 829448 | tf_op jit(solution)/shard_map/ppermute | solution.py:547
  238.6 31.1 %collective-permute-start.9 = (bf16[3,180,256]{2,1,0:T(8,128)(2,1)S(1)}, bf16[3,180,256]{2,1,0:T(8,128)(2,1)}, u32[]{:S(2)}, u32[]{:S(2)}) collective-permute-start(bf16[3,180,256]{2,1,0:T(8,128)(2,1)S(1)} %get-tuple-element.155), channel_id=1, source_target_pairs={{0,4},{1,5},{2,6},{3,7},{4,0},{5,1},{6,2},{7,3},{8,12},{9,13},{10,... | collective-permute-start | bytes 829448 | tf_op jit(solution)/shard_map/ppermute | solution.py:547
  247.2 30.2 %copy-start.28 = (bf16[3,180,256]{2,1,0:T(8,128)(2,1)}, bf16[3,180,256]{2,1,0:T(8,128)(2,1)S(1)}, u32[]{:S(2)}) copy-start(bf16[3,180,256]{2,1,0:T(8,128)(2,1)S(1)} %collective-permute-done.10.refs_5_) | copy-start | bytes 829444
  277.4 24.3 %copy-start.13 = (s32[4]{0:T(128)S(1)}, s32[4]{0:T(128)}, u32[]{:S(2)}) copy-start(s32[4]{0:T(128)} %copy-done.12) | copy-start | bytes 52
  277.4 24.3 %all-to-all-start.6 = ((bf16[32,72,128]{2,1,0:T(8,128)(2,1)}), bf16[32,72,128]{2,1,0:T(8,128)(2,1)}, u32[]{:S(2)}, u32[]{:S(2)}) async-start(bf16[32,72,128]{2,1,0:T(8,128)(2,1)} %shard_map.102), calls=%async_computation.6 | async-start | bytes 1179648 | tf_op jit(solution)/shard_map/all_to_all | solution.py:24
  285.3 42.2 %copy-start.2 = (f32[768,128]{1,0:T(8,128)S(1)}, f32[768,128]{1,0:T(8,128)}, u32[]{:S(2)}) copy-start(f32[768,128]{1,0:T(8,128)} %broadcast_in_dim.28.lat_w) | copy-start | bytes 1179652
  285.4 2.7 collective-permute-start.11
  286.3 8.9 %collective-permute-start.12 = (bf16[3,180,256]{2,1,0:T(8,128)(2,1)S(1)}, bf16[3,180,256]{2,1,0:T(8,128)(2,1)S(1)}, u32[]{:S(2)}, u32[]{:S(2)}) collective-permute-start(bf16[3,180,256]{2,1,0:T(8,128)(2,1)S(1)} %get-tuple-element.152), channel_id=1, source_target_pairs={{0,3},{1,2},{2,1},{3,0},{4,7},{5,6},{6,5},{7,4},{8,11},{9,10},{10,... | collective-permute-start | bytes 829448 | tf_op jit(solution)/shard_map/ppermute | solution.py:547
  286.6 10.4 %collective-permute-start.13 = (bf16[3,180,256]{2,1,0:T(8,128)(2,1)S(1)}, bf16[3,180,256]{2,1,0:T(8,128)(2,1)}, u32[]{:S(2)}, u32[]{:S(2)}) collective-permute-start(bf16[3,180,256]{2,1,0:T(8,128)(2,1)S(1)} %get-tuple-element.151), channel_id=1, source_target_pairs={{0,7},{1,6},{2,5},{3,4},{4,3},{5,2},{6,1},{7,0},{8,15},{9,14},{10,... | collective-permute-start | bytes 829448 | tf_op jit(solution)/shard_map/ppermute | solution.py:547
  288.1 42.3 %copy-start.31 = (bf16[3,180,256]{2,1,0:T(8,128)(2,1)}, bf16[3,180,256]{2,1,0:T(8,128)(2,1)S(1)}, u32[]{:S(2)}) copy-start(bf16[3,180,256]{2,1,0:T(8,128)(2,1)S(1)} %collective-permute-done.11.refs_1_) | copy-start | bytes 829444
  301.7 25.9 %copy-start.6 = (bf16[2,768,640]{2,1,0:T(8,128)(2,1)S(1)}, bf16[2,768,640]{2,1,0:T(8,128)(2,1)}, u32[]{:S(2)}) copy-start(bf16[2,768,640]{2,1,0:T(8,128)(2,1)} %copy-done.4) | copy-start | bytes 5898244
  330.4 51.6 %all-to-all-start.8 = ((bf16[256,24,128]{2,1,0:T(8,128)(2,1)}), bf16[256,24,128]{2,1,0:T(8,128)(2,1)S(1)}, u32[]{:S(2)}, u32[]{:S(2)}) async-start(bf16[256,24,128]{2,1,0:T(8,128)(2,1)} %shard_map.104), calls=%async_computation.8 | async-start | bytes 3145728 | tf_op jit(solution)/shard_map/all_to_all | solution.py:24
  340.3 55.6 %reduce-scatter.2.cloned.1.call-start = ((), (), s32[]{:S(2)}) async-start(), calls=%async_computation.11 | async-start | bytes 2359296 | tf_op jit(solution)/shard_map/reduce_scatter | solution.py:738
  390.5 33.5 %all-to-all-start.9 = ((bf16[8,3,180,256]{3,2,1,0:T(8,128)(2,1)}), bf16[8,3,180,256]{3,2,1,0:T(8,128)(2,1)S(1)}, u32[]{:S(2)}, u32[]{:S(2)}) async-start(bf16[8,3,180,256]{3,2,1,0:T(8,128)(2,1)} %shard_map.105), calls=%async_computation.9 | async-start | bytes 4521984 | tf_op jit(solution)/shard_map/all_to_all | solution.py:24
  (24 other events, 116.5 us)
Sparse Core Ops, SparseCore 0:
  344.2 38.5 reduce-scatter.1
